TPU v7x, 32 devices: a whole 2x2x4 slice. The times are simulated.
32 devices in a mesh: tok: 16 (over z, y, core), col: 2 (over x).
Axes of the slice: x: 2, y: 2, z: 4, core: 2. Of those that a mesh axis runs over, the one named last changes fastest.
Arguments:
- activations: bfloat16 [16384, 4096], P('tok'), may hold values from -14 to 14
- targets: bfloat16 [16384, 4096], P('tok', 'col'), may hold values from -20 to 20
- map_weight: float32 [4096, 4096], P('tok', 'col'), may hold values from -1 to 2
- first_moment: float32 [4096, 4096], P('tok', 'col'), may hold values from -0.12 to 0.12
- second_moment: float32 [4096, 4096], P('tok', 'col'), may hold values from 0.0001 to 0.001
- down_weight: bfloat16 [14336, 4096], P('tok', 'col'), may hold values from -6 to 6
Outputs:
- new_map: float32 [4096, 4096], P('tok', 'col')
- joined: bfloat16 [14336, 4096], P('tok', 'col')
All inputs are finite; a program needn't handle non-finite values.
Results may differ from a plain program's by a relative error of at most 0.0041.
The roundings to bfloat16 on the way count: a program that leaves them out, or rounds other values in their place, can miss the bound.
Values may be sent and summed in bfloat16 or wider, within the bound.
A program may use at most 128 MiB of HBM per device.

v0:
```python
import jax
import jax.numpy as jnp
from jax import lax
from jax.sharding import PartitionSpec as P


def adam_step(weight, first, second, grad):
    moment1 = 0.9 * first + 0.1 * grad
    moment2 = 0.95 * second + 0.05 * grad * grad
    return weight - 0.02 * (moment1 / (1.0 - 0.9**10)) / (
        jnp.sqrt(moment2 / (1.0 - 0.95**10)) + 1e-08
    )


def per_device(activations, targets, map_weight, first_moment, second_moment, down_weight):
    down_full = None
    target32 = targets.astype(jnp.float32)
    map_half = map_weight.astype(jnp.bfloat16)
    block = activations
    predicted = jnp.dot(
        block,
        lax.all_gather(map_half, "tok", axis=0, tiled=True),
        preferred_element_type=jnp.float32,
    )
    inner, pred_sq, target_sq = lax.psum(
        (
            jnp.sum(predicted * target32, axis=1),
            jnp.sum(predicted * predicted, axis=1),
            jnp.sum(target32 * target32, axis=1),
        ),
        "col",
    )
    pred_norm = jnp.sqrt(pred_sq + 1e-06)
    targ_norm = jnp.sqrt(target_sq + 1e-06)
    scale = 1.0 / (pred_norm * targ_norm)
    coef = inner * scale / (pred_norm * pred_norm)
    d_pred = (coef[:, None] * predicted - scale[:, None] * target32).astype(jnp.bfloat16)
    block = activations
    grad = lax.psum_scatter(
        lax.dot_general(
            block, d_pred, (((0,), (0,)), ((), ())), preferred_element_type=jnp.float32
        ),
        "tok",
        scatter_dimension=0,
        tiled=True,
    )
    new_map = adam_step(map_weight, first_moment, second_moment, grad)
    down_full = lax.all_gather(down_weight, "col", axis=1, tiled=True)
    block = down_full
    joined = jnp.dot(
        block,
        lax.all_gather(new_map.astype(jnp.bfloat16), "tok", axis=0, tiled=True),
        preferred_element_type=jnp.float32,
    )
    return (new_map, joined.astype(jnp.bfloat16))


def solution(mesh):
    in_specs = (
        P("tok", None),
        P("tok", "col"),
        P("tok", "col"),
        P("tok", "col"),
        P("tok", "col"),
        P("tok", "col"),
    )
    out_specs = (P("tok", "col"), P("tok", "col"))
    return jax.shard_map(
        per_device, mesh=mesh, in_specs=in_specs, out_specs=out_specs, check_vma=False
    )
```

profile of v0, /device:TPU:0, one launch (start us, length us, event | category | flops | bytes accessed | tf_op | source)
XLA Modules:
  0.0 703.1 jit_solution(10327395969240151011)
XLA Ops:
  8.0 0.0 all-gather.4.cloned.1.call-start
  8.0 2.7 convert_element_type.18
  10.8 0.0 all-gather.4.cloned.1.call-update
  10.8 0.0 reduce-scatter.2.cloned.1.call-start
  10.8 130.4 %all-gather.4.cloned.1.call-done = bf16[4096,2048]{1,0:T(8,128)(2,1)} async-done(((bf16[256,2048]{1,0:T(8,128)(2,1)}), bf16[4096,2048]{1,0:T(8,128)(2,1)}) %all-gather.4.cloned.1.call-update) | async-done | bytes 16777232 | tf_op jit(solution)/shard_map/all_gather | solution.py:22
  141.2 25.1 %fusion = (f32[1024]{0:T(1024)S(1)}, f32[1024]{0:T(1024)S(1)}, f32[1024]{0:T(1024)S(1)}, f32[1024,2048]{1,0:T(8,128)}) fusion(bf16[1024,2048]{1,0:T(8,128)(2,1)} %param.7, bf16[1024,4096]{1,0:T(8,128)(2,1)} %param.6, bf16[4096,2048]{1,0:T(8,128)(2,1)} %all-gather.4.cloned.1.call-done), kind=kOutput, calls=%fused_computation.4 | convolution fusion | flops 17194549248 | bytes 37761024 | tf_op jit(solution)/shard_map/dot_general | solution.py:20
  166.3 8.0 %all-reduce = (f32[1024]{0:T(1024)S(1)}, f32[1024]{0:T(1024)S(1)}, f32[1024]{0:T(1024)S(1)}) all-reduce(f32[1024]{0:T(1024)S(1)} %get-tuple-element.6, f32[1024]{0:T(1024)S(1)} %get-tuple-element.5, f32[1024]{0:T(1024)S(1)} %get-tuple-element.4), channel_id=1, replica_groups=mesh['tok'=16,'col'=2] {'col'}, use_global_device_ids=true, to_apply=%region_5.0 | all-reduce | flops 3072 | bytes 24576 | tf_op jit(solution)/shard_map/psum | solution.py:25
  174.4 26.6 %convolution_bitcast_fusion = f32[4096,2048]{0,1:T(8,128)} fusion(bf16[1024,4096]{1,0:T(8,128)(2,1)} %param.6, bf16[1024,2048]{1,0:T(8,128)(2,1)} %param.7, f32[1024,2048]{1,0:T(8,128)} %get-tuple-element.14, f32[1024]{0:T(1024)S(1)} %get-tuple-element.13, f32[1024]{0:T(1024)S(1)} %get-tuple-element.12), kind=kOutput, calls=%fused_computation | convolution fusion | flops 17190354944 | bytes 54534144 | tf_op jit(solution)/shard_map/dot_general | solution.py:40
  201.0 0.0 reduce-scatter.2.cloned.1.call-update
  201.0 0.0 copy-start
  201.0 0.0 all-gather.8.cloned.1.call-start
  201.1 0.5 all-gather.8.cloned.1.call-update
  201.6 0.2 all-gather.6.cloned.1.call-start
  201.8 0.8 copy-done
  202.6 1.8 copy.10
  204.4 0.0 copy-start.1
  204.4 3.2 copy.8
  207.6 0.0 copy-done.1
  207.6 2.6 copy.9
  210.2 321.0 %reduce-scatter.2.cloned.1.call-done = f32[256,2048]{0,1:T(8,128)} async-done(((f32[4096,2048]{0,1:T(8,128)}), f32[256,2048]{0,1:T(8,128)}) %reduce-scatter.2.cloned.1.call-update) | async-done | bytes 2097168 | tf_op jit(solution)/shard_map/reduce_scatter | solution.py:39
  531.2 5.8 fusion.13
  537.0 0.0 all-gather.6.cloned.1.call-update
  537.0 1.8 copy.11
  538.9 0.0 all-gather.8.cloned.1.call-done
  538.9 127.3 %all-gather.6.cloned.1.call-done = bf16[4096,2048]{0,1:T(8,128)(2,1)} async-done(((bf16[256,2048]{0,1:T(8,128)(2,1)}), bf16[4096,2048]{0,1:T(8,128)(2,1)}) %all-gather.6.cloned.1.call-update) | async-done | bytes 16777232 | tf_op jit(solution)/shard_map/all_gather | solution.py:52
  666.2 23.4 %convert_bitcast_fusion = bf16[896,2048]{0,1:T(8,128)(2,1)} fusion(bf16[4096,2048]{0,1:T(8,128)(2,1)} %all-gather.6.cloned.1.call-done, bf16[896,4096]{1,0:T(8,128)(2,1)} %all-gather.8.cloned.1.call-done), kind=kOutput, calls=%fused_computation.11 | convolution fusion | flops 15034220544 | bytes 27787264 | tf_op jit(solution)/shard_map/dot_general | solution.py:50
  689.6 6.0 copy.12
  (1 shorter events, 0.0 us)
Async XLA Ops:
  8.0 133.2 %all-gather.4.cloned.1.call-start = ((), (), s32[]{:S(2)}) async-start(), calls=%async_computation.1 | async-start | bytes 17825792 | tf_op jit(solution)/shard_map/all_gather | solution.py:22
  10.8 520.4 %reduce-scatter.2.cloned.1.call-start = ((), (), s32[]{:S(2)}) async-start(), calls=%async_computation.2 | async-start | bytes 35651584 | tf_op jit(solution)/shard_map/reduce_scatter | solution.py:39
  201.0 1.6 copy-start
  201.0 337.9 %all-gather.8.cloned.1.call-start = ((), (), s32[]{:S(2)}) async-start(), calls=%async_computation.4 | async-start | bytes 11010048 | tf_op jit(solution)/shard_map/all_gather | solution.py:48
  201.6 464.6 %all-gather.6.cloned.1.call-start = ((), (), s32[]{:S(2)}) async-start(), calls=%async_computation.3 | async-start | bytes 17825792 | tf_op jit(solution)/shard_map/all_gather | solution.py:52
  204.4 3.2 copy-start.1
Sparse Core Ops, SparseCore 0:
  11.6 129.5 all-gather.3
  201.1 330.0 reduce-scatter.1
Sparse Core Ops, SparseCore 1:
  203.0 89.3 all-gather.7
  537.1 129.0 all-gather.5
where the time goes:
time: 703 us
  waiting for transfers between devices  579 us (82%)
  matrix products  75.1 us (11%)
  local copies, waits for them, and re-layouts  16.2 us (2%)
  between operations  15.5 us (2%)
  other arithmetic  8.57 us (1%)
  blocking collectives  8.04 us (1%)
    reduce_scatter x1, waiting for transfers between devices, per_device(): lax.psum_scatter(lax.dot_general(block, d_pred, (((0,), (0,)), ((), ())),...  321 us
    all_gather x1, waiting for transfers between devices, per_device(): lax.all_gather(map_half, 'tok', axis=0, tiled=True)  130 us
    all_gather x1, waiting for transfers between devices, per_device(): lax.all_gather(new_map.astype(jnp.bfloat16), 'tok', axis=0, tiled=True)  127 us
    dot_general x1, matrix products, per_device(): lax.dot_general(block, d_pred, (((0,), (0,)), ((), ())), preferred_elemen...  26.6 us
    dot_general x1, matrix products, per_device(): jnp.dot(block, lax.all_gather(map_half, 'tok', axis=0, tiled=True), prefe...  25.1 us
    dot_general x1, matrix products, per_device(): jnp.dot(block, lax.all_gather(new_map.astype(jnp.bfloat16), 'tok', axis=0...  23.4 us
    unnamed x9, local copies, waits for them, and re-layouts  16.2 us
  transfers between devices with their start and end apart: 4, of which 3 were waited for; matrix products, arithmetic and copies ran while one was open for 2% of the time, Pallas kernels for 0%

commit v1 on v0

v1 whole, which is shorter than its diff:
```python
import functools

import jax
import jax.numpy as jnp
from jax import lax
from jax.experimental import pallas as pl
from jax.experimental.pallas import tpu as pltpu
from jax.sharding import PartitionSpec as P

BF16 = jnp.bfloat16
F32 = jnp.float32
MESH = pl.DeviceIdType.MESH
VMEM_BYTES = 60 * 1024 * 1024


def place():
    me = lax.axis_index("tok")
    return me // 4, lax.rem(me // 2, 2), lax.rem(me, 2)


def meet(line):
    a, b, c = place()
    barrier = pltpu.get_barrier_semaphore()
    left, right = lax.rem(a + line - 1, line), lax.rem(a + 1, line)
    for t in (
        4 * left + 2 * b + c,
        4 * right + 2 * b + c,
        4 * a + 2 * (1 - b) + c,
        4 * a + 2 * b + 1 - c,
    ):
        pl.semaphore_signal(barrier, inc=1, device_id={"tok": t}, device_id_type=MESH)
    pl.semaphore_wait(barrier, 4)


def remote(src, dst, send, recv, tok):
    return pltpu.make_async_remote_copy(
        src_ref=src, dst_ref=dst, send_sem=send, recv_sem=recv,
        device_id={"tok": tok}, device_id_type=MESH,
    )


def gather_dot_kernel(
    line, lhs_ref, shard_ref, out_ref, held, lhs, acc,
    lhs_sem, own_sem, recv, left_sem, right_sem, y_sem, core_sem,
):
    a, b, c = place()
    depth, width = shard_ref.shape
    tile = min(256, width)

    def slot(x, y, z):
        return 4 * x + 2 * y + z

    def lhs_copy(s):
        columns = pl.ds(pl.multiple_of(s * depth, depth), depth)
        return pltpu.make_async_copy(lhs_ref.at[:, columns], lhs.at[s], lhs_sem.at[s])

    own = pltpu.make_async_copy(shard_ref, held.at[slot(a, b, c)], own_sem)
    own.start()

    @pl.loop(0, 4 * line)
    def _(s):
        lhs_copy(s).start()

    acc[...] = jnp.zeros_like(acc)
    meet(line)
    own.wait()

    def send(s, sem, tok):
        return remote(held.at[s], held.at[s], sem.at[s], recv.at[s], tok)

    def to_left(x):
        return send(slot(x, b, c), left_sem, slot(a - 1, b, c))

    def to_right(x):
        return send(slot(x, b, c), right_sem, slot(a + 1, b, c))

    def to_row(x):
        return send(slot(x, b, c), y_sem, slot(a, 1 - b, c))

    def to_core(x, y):
        return send(slot(x, y, c), core_sem, slot(a, b, 1 - c))

    def arrived(s):
        send(s, core_sem, slot(a, b, 1 - c)).wait_recv()

    def multiply(s):
        lhs_copy(s).wait()

        @pl.loop(0, width // tile)
        def _(n):
            columns = pl.ds(pl.multiple_of(n * tile, tile), tile)
            acc[:, columns] += jnp.dot(
                lhs[s], held[s, :, columns], preferred_element_type=F32
            )

    def each(d, work):
        for sign in (-1, 1):
            x = a + sign * d
            inside = (x >= 0) & (x < line) & (d >= 0) & ((d > 0) | (sign < 0))
            pl.when(inside)(functools.partial(work, x))

    def line_in(x):
        @pl.when(x != a)
        def _():
            arrived(slot(x, b, c))

        @pl.when((x <= a) & (a < line - 1))
        def _():
            to_right(x).start()

        @pl.when((x >= a) & (a > 0))
        def _():
            to_left(x).start()

        to_row(x).start()
        to_core(x, b).start()

    def row_in(x):
        arrived(slot(x, 1 - b, c))
        to_core(x, 1 - b).start()
        multiply(slot(x, 1 - b, c))

    def core_in(y, x):
        arrived(slot(x, y, 1 - c))
        multiply(slot(x, y, 1 - c))

    @pl.loop(0, line + 1)
    def _(d):
        each(d, line_in)
        each(d, lambda x: multiply(slot(x, b, c)))
        each(d - 1, functools.partial(core_in, b))
        each(d - 1, row_in)
        each(d - 2, functools.partial(core_in, 1 - b))

    each(line - 1, functools.partial(core_in, 1 - b))

    @pl.loop(0, line)
    def _(x):
        @pl.when((x <= a) & (a < line - 1))
        def _():
            to_right(x).wait_send()

        @pl.when((x >= a) & (a > 0))
        def _():
            to_left(x).wait_send()

        to_row(x).wait_send()
        to_core(x, b).wait_send()
        to_core(x, 1 - b).wait_send()

    out_ref[...] = acc[...].astype(out_ref.dtype)


def gather_dot(lhs, shard, tok, dtype, collective):
    rows = lhs.shape[0]
    depth, width = shard.shape
    dma = pltpu.SemaphoreType.DMA
    return pl.pallas_call(
        functools.partial(gather_dot_kernel, tok // 4),
        out_shape=jax.ShapeDtypeStruct((rows, width), dtype),
        in_specs=[pl.BlockSpec(memory_space=pl.ANY)] * 2,
        out_specs=pl.BlockSpec(memory_space=pltpu.VMEM),
        scratch_shapes=[
            pltpu.VMEM((tok, depth, width), BF16),
            pltpu.VMEM((tok, rows, depth), BF16),
            pltpu.VMEM((rows, width), F32),
            dma((tok,)), dma, dma((tok,)), dma((tok,)), dma((tok,)), dma((tok,)), dma((tok,)),
        ],
        compiler_params=pltpu.CompilerParams(
            collective_id=collective, has_side_effects=True, vmem_limit_bytes=VMEM_BYTES
        ),
        cost_estimate=pl.CostEstimate(
            flops=2 * rows * width * depth * tok,
            bytes_accessed=2 * rows * depth * tok + 4 * rows * width,
            transcendentals=0,
        ),
    )(lhs, shard)


def dot_scatter_kernel(
    line, act_ref, grad_ref, out_ref,
    core_out, core_in, row_out, row_in, line_out, from_left, from_right,
    core_send, core_recv, row_send, row_recv, line_send, left_recv, right_recv,
):
    a, b, c = place()
    depth, width = out_ref.shape
    tile = min(512, width)
    meet(line)

    def slot(x, y, z):
        return 4 * x + 2 * y + z

    def tiles(work):
        @pl.loop(0, width // tile)
        def _(n):
            work(pl.ds(pl.multiple_of(n * tile, tile), tile))

    def part(s, columns):
        rows = pl.ds(pl.multiple_of(s * depth, depth), depth)
        return lax.dot_general(
            act_ref[:, rows], grad_ref[:, columns], (((0,), (0,)), ((), ())),
            preferred_element_type=F32,
        )

    def core_copy(k):
        return remote(
            core_out.at[k], core_in.at[k], core_send.at[k], core_recv.at[k], slot(a, b, 1 - c)
        )

    def row_copy(x):
        return remote(
            row_out.at[x], row_in.at[x], row_send.at[x], row_recv.at[x], slot(a, 1 - b, c)
        )

    def right_copy(x):
        return remote(
            line_out.at[x], from_left.at[x], line_send.at[x], left_recv.at[x],
            slot(a + 1, b, c),
        )

    def left_copy(x):
        return remote(
            line_out.at[x], from_right.at[x], line_send.at[x], right_recv.at[x],
            slot(a - 1, b, c),
        )

    def each(d, work):
        for sign in (-1, 1):
            x = a + sign * d
            inside = (x >= 0) & (x < line) & (d >= 0) & ((d > 0) | (sign < 0))
            pl.when(inside)(functools.partial(work, x))

    def give_core(y, x):
        k = 2 * x + y

        def work(columns):
            core_out[k, :, columns] = part(slot(x, y, 1 - c), columns).astype(BF16)

        tiles(work)
        core_copy(k).start()

    def give_row(x):
        k = 2 * x + 1 - b
        core_copy(k).wait_recv()

        def work(columns):
            total = part(slot(x, 1 - b, c), columns) + core_in[k, :, columns].astype(F32)
            row_out[x, :, columns] = total.astype(BF16)

        tiles(work)
        row_copy(x).start()

    def total_of(x, columns):
        k = 2 * x + b
        return (
            part(slot(x, b, c), columns)
            + core_in[k, :, columns].astype(F32)
            + row_in[x, :, columns].astype(F32)
        )

    def give_line(x):
        core_copy(2 * x + b).wait_recv()
        row_copy(x).wait_recv()

        def first(columns):
            out_ref[:, columns] = total_of(x, columns)

        tiles(first)

        @pl.when((x >= a) & (a > 0))
        def _():
            right_copy(x).wait_recv()
            tiles(functools.partial(add, from_left, x))

        @pl.when((x <= a) & (a < line - 1))
        def _():
            left_copy(x).wait_recv()
            tiles(functools.partial(add, from_right, x))

        @pl.when(x != a)
        def _():
            def cast(columns):
                line_out[x, :, columns] = out_ref[:, columns].astype(BF16)

            tiles(cast)

        @pl.when(x > a)
        def _():
            right_copy(x).start()

        @pl.when(x < a)
        def _():
            left_copy(x).start()

    def add(ref, x, columns):
        out_ref[:, columns] += ref[x, :, columns].astype(F32)

    @pl.loop(0, line + 1)
    def _(i):
        d = line - 1 - i
        each(d, functools.partial(give_core, 1 - b))
        each(d, give_row)
        each(d, functools.partial(give_core, b))

        @pl.when(i > 0)
        def _():
            each(d + 1, give_line)

    @pl.loop(0, line)
    def _(x):
        core_copy(2 * x).wait_send()
        core_copy(2 * x + 1).wait_send()
        row_copy(x).wait_send()

        @pl.when(x > a)
        def _():
            right_copy(x).wait_send()

        @pl.when(x < a)
        def _():
            left_copy(x).wait_send()


def dot_scatter(activations, d_pred, tok, collective):
    tokens, features = activations.shape
    width = d_pred.shape[1]
    depth = features // tok
    line = tok // 4
    dma = pltpu.SemaphoreType.DMA

    def slots(n):
        return pltpu.VMEM((n, depth, width), BF16)

    return pl.pallas_call(
        functools.partial(dot_scatter_kernel, line),
        out_shape=jax.ShapeDtypeStruct((depth, width), F32),
        in_specs=[pl.BlockSpec(memory_space=pltpu.VMEM)] * 2,
        out_specs=pl.BlockSpec(memory_space=pltpu.VMEM),
        scratch_shapes=[
            slots(2 * line), slots(2 * line), slots(line), slots(line), slots(line),
            slots(line), slots(line),
            dma((2 * line,)), dma((2 * line,)), dma((line,)), dma((line,)), dma((line,)),
            dma((line,)), dma((line,)),
        ],
        compiler_params=pltpu.CompilerParams(
            collective_id=collective, has_side_effects=True, vmem_limit_bytes=VMEM_BYTES
        ),
        cost_estimate=pl.CostEstimate(
            flops=2 * tokens * features * width,
            bytes_accessed=2 * tokens * (features + width),
            transcendentals=0,
        ),
    )(activations, d_pred)


def adam_step(weight, first, second, grad):
    moment1 = 0.9 * first + 0.1 * grad
    moment2 = 0.95 * second + 0.05 * grad * grad
    return weight - 0.02 * (moment1 / (1.0 - 0.9**10)) / (
        jnp.sqrt(moment2 / (1.0 - 0.95**10)) + 1e-08
    )


def per_device(tok, activations, targets, map_weight, first_moment, second_moment, down_weight):
    target32 = targets.astype(F32)
    down_full = lax.all_gather(down_weight, "col", axis=1, tiled=True)
    predicted = gather_dot(activations, map_weight.astype(BF16), tok, F32, 1)
    sums = lax.psum(
        jnp.stack(
            [
                jnp.sum(predicted * target32, axis=1),
                jnp.sum(predicted * predicted, axis=1),
                jnp.sum(target32 * target32, axis=1),
            ]
        ),
        "col",
    )
    inner, pred_sq, target_sq = sums[0], sums[1], sums[2]
    pred_norm = jnp.sqrt(pred_sq + 1e-06)
    targ_norm = jnp.sqrt(target_sq + 1e-06)
    scale = 1.0 / (pred_norm * targ_norm)
    coef = inner * scale / (pred_norm * pred_norm)
    d_pred = (coef[:, None] * predicted - scale[:, None] * target32).astype(BF16)
    grad = dot_scatter(activations, d_pred, tok, 2)
    new_map = adam_step(map_weight, first_moment, second_moment, grad)
    joined = gather_dot(down_full, new_map.astype(BF16), tok, BF16, 3)
    return (new_map, joined)


def solution(mesh):
    split = P("tok", "col")
    return jax.shard_map(
        functools.partial(per_device, mesh.shape["tok"]),
        mesh=mesh,
        in_specs=(P("tok", None),) + (split,) * 5,
        out_specs=(split, split),
        check_vma=False,
    )
```

time: 703 us -> 378 us (0.54)
  waiting for transfers between devices: 579 us -> 0.68 us
  Pallas kernels: 0 us -> 330 us
  matrix products: 75.1 us -> 0 us
  other arithmetic: 8.57 us -> 19.8 us
  local copies, waits for them, and re-layouts: 16.2 us -> 5.22 us
    pallas_call x0 -> x3, Pallas kernels: none -> 330 us  [the longest x2 221 us: gather_dot(): pl.pallas_call(functools.partial(gather_dot_kernel, tok // 4), out_shape=...]
    reduce_scatter x1 -> x0, waiting for transfers between devices: 321 us -> none  [per_device(): lax.psum_scatter(lax.dot_general(block, d_pred, (((0,), (0,)), ((), ())),...]
    all_gather x2 -> x0, waiting for transfers between devices: 258 us -> none  [the longest x1 130 us: per_device(): lax.all_gather(map_half, 'tok', axis=0, tiled=True)]
    dot_general x3 -> x0, matrix products: 75.1 us -> none  [the longest x1 26.6 us: per_device(): lax.dot_general(block, d_pred, (((0,), (0,)), ((), ())), preferred_elemen...]
    unnamed x9 -> x3, local copies, waits for them, and re-layouts: 16.2 us -> 5.22 us
  transfers between devices with their start and end apart: 4 -> 1, of which waited for: 3 -> 0; matrix products, arithmetic and copies ran while one was open for 2% -> 5% of each run, Pallas kernels for 0% -> 58%
where the time goes in v1:
time: 378 us
  Pallas kernels  330 us (87%)
  other arithmetic  19.8 us (5%)
  between operations  14.1 us (4%)
  blocking collectives  8.15 us (2%)
  local copies, waits for them, and re-layouts  5.22 us (1%)
    pallas_call x2, Pallas kernels, gather_dot(): pl.pallas_call(functools.partial(gather_dot_kernel, tok // 4), out_shape=...  221 us
    pallas_call x1, Pallas kernels, dot_scatter(): pl.pallas_call(functools.partial(dot_scatter_kernel, line), out_shape=jax...  109 us
    psum x1, blocking collectives, per_device(): lax.psum(jnp.stack([jnp.sum(predicted * target32, axis=1), jnp.sum(predic...  8.15 us
  transfers between devices with their start and end apart: 1, of which 0 were waited for; matrix products, arithmetic and copies ran while one was open for 5% of the time, Pallas kernels for 58%

profile of v1, /device:TPU:0, one launch (start us, length us, event | category | flops | bytes accessed | tf_op | source)
XLA Modules:
  0.0 378.0 jit_solution(5386576171853400591)
XLA Ops:
  7.2 0.0 copy-start
  7.2 0.0 all-gather.2.cloned.1.call-start
  7.2 0.7 all-gather.2.cloned.1.call-update
  7.9 0.8 copy-done
  8.8 1.1 convert_element_type.12.shard_ref
  9.9 110.8 %shard_map.77 = f32[1024,2048]{1,0:T(8,128)} custom-call(bf16[1024,4096]{1,0:T(8,128)(2,1)} %act_ref.1, bf16[256,2048]{1,0:T(8,128)(2,1)} %convert_element_type.12.shard_ref), custom_call_target="tpu_custom_call" | custom-call | flops 17179869184 | bytes 16777216 | tf_op jit(solution)/shard_map/pallas_call | solution.py:158
  120.7 5.8 %fusion = (f32[1024]{0:T(1024)S(1)}, f32[1024]{0:T(1024)S(1)}, f32[1024]{0:T(1024)S(1)}) fusion(f32[1024,2048]{1,0:T(8,128)} %shard_map.77, bf16[1024,2048]{1,0:T(8,128)(2,1)} %param.7), kind=kLoop, calls=%fused_computation.3 | loop fusion | flops 14676992 | bytes 12595200 | tf_op jit(solution)/shard_map/reduce_sum | solution.py:371
  126.5 8.1 %psum.7 = f32[3,1024]{1,0:T(4,128)S(1)} all-reduce(f32[3,1024]{1,0:T(4,128)S(1)} %pad_maximum_fusion), channel_id=1, replica_groups=mesh['tok'=16,'col'=2] {'col'}, use_global_device_ids=true, to_apply=%region_3.0 | all-reduce | flops 3072 | bytes 24576 | tf_op jit(solution)/shard_map/psum | solution.py:368
  134.7 6.9 %fusion.3.grad_ref = bf16[1024,2048]{1,0:T(8,128)(2,1)} fusion(bf16[1024,2048]{1,0:T(8,128)(2,1)} %param.7, f32[1024,2048]{1,0:T(8,128)} %shard_map.77, f32[1024]{0:T(1024)S(1)} %bitcast.7, f32[1024]{0:T(1024)S(1)} %multiply_divide_fusion), kind=kLoop, calls=%fused_computation.6 | loop fusion | flops 10485760 | bytes 16785408 | tf_op jit(solution)/shard_map/convert_element_type | solution.py:383
  141.7 108.6 %shard_map.78 = f32[256,2048]{1,0:T(8,128)} custom-call(bf16[1024,4096]{1,0:T(8,128)(2,1)} %act_ref.1, bf16[1024,2048]{1,0:T(8,128)(2,1)} %fusion.3.grad_ref), custom_call_target="tpu_custom_call" | custom-call | flops 17179869184 | bytes 12582912 | tf_op jit(solution)/shard_map/pallas_call | solution.py:334
  250.3 5.9 %fusion.15 = (bf16[256,2048]{1,0:T(8,128)(2,1)}, f32[256,2048]{1,0:T(8,128)}) fusion(f32[256,2048]{1,0:T(8,128)S(1)} %copy-done, f32[256,2048]{1,0:T(8,128)} %shard_map.78, f32[256,2048]{1,0:T(8,128)} %param.10, f32[256,2048]{1,0:T(8,128)} %param.9), kind=kLoop, calls=%fused_computation.24 | loop fusion | flops 6815744 | bytes 11534336 | tf_op jit(solution)/shard_map/convert_element_type | solution.py:386
  256.2 0.0 all-gather.2.cloned.1.call-done.lhs_ref
  256.2 110.6 %shard_map.79 = bf16[896,2048]{1,0:T(8,128)(2,1)} custom-call(bf16[896,4096]{1,0:T(8,128)(2,1)} %all-gather.2.cloned.1.call-done.lhs_ref, bf16[256,2048]{1,0:T(8,128)(2,1)} %get-tuple-element.5.shard_ref), custom_call_target="tpu_custom_call" | custom-call | flops 15032385536 | bytes 14680064 | tf_op jit(solution)/shard_map/pallas_call | solution.py:158
  366.8 4.4 %copy.9 = bf16[896,2048]{1,0:T(8,128)(2,1)} copy(bf16[896,2048]{1,0:T(8,128)(2,1)} %shard_map.79) | data formatting | bytes 7340032
  (3 shorter events, 0.1 us)
Async XLA Ops:
  7.2 1.6 copy-start
  7.2 249.1 %all-gather.2.cloned.1.call-start = ((), (), s32[]{:S(2)}) async-start(), calls=%async_computation | async-start | bytes 11010048 | tf_op jit(solution)/shard_map/all_gather | solution.py:366
Sparse Core Ops, SparseCore 0:
  9.6 94.8 all-gather.1

commit v2 on v1

v2 whole, which is shorter than its diff:
```python
import functools

import jax
import jax.numpy as jnp
from jax import lax
from jax.experimental import pallas as pl
from jax.experimental.pallas import tpu as pltpu
from jax.sharding import PartitionSpec as P

BF16 = jnp.bfloat16
F32 = jnp.float32
MESH = pl.DeviceIdType.MESH
PIECES = 2
VMEM_BYTES = 60 * 1024 * 1024


def place():
    me = lax.axis_index("tok")
    return me // 4, lax.rem(me // 2, 2), lax.rem(me, 2)


def meet(line):
    a, b, c = place()
    barrier = pltpu.get_barrier_semaphore()
    left, right = lax.rem(a + line - 1, line), lax.rem(a + 1, line)
    for t in (
        4 * left + 2 * b + c,
        4 * right + 2 * b + c,
        4 * a + 2 * (1 - b) + c,
        4 * a + 2 * b + 1 - c,
    ):
        pl.semaphore_signal(barrier, inc=1, device_id={"tok": t}, device_id_type=MESH)
    pl.semaphore_wait(barrier, 4)


def remote(src, dst, send, recv, tok):
    return pltpu.make_async_remote_copy(
        src_ref=src, dst_ref=dst, send_sem=send, recv_sem=recv,
        device_id={"tok": tok}, device_id_type=MESH,
    )


def gather_dot_kernel(
    line, lhs_ref, shard_ref, out_ref, held, lhs, acc,
    lhs_sem, own_sem, recv, left_sem, right_sem, y_sem, core_sem,
):
    a, b, c = place()
    depth, width = shard_ref.shape
    piece = width // PIECES
    tile = min(256, piece)

    def slot(x, y, z):
        return 4 * x + 2 * y + z

    def lhs_copy(s):
        columns = pl.ds(pl.multiple_of(s * depth, depth), depth)
        return pltpu.make_async_copy(lhs_ref.at[:, columns], lhs.at[s], lhs_sem.at[s])

    def own(p):
        columns = pl.ds(p * piece, piece)
        return pltpu.make_async_copy(
            shard_ref.at[:, columns], held.at[slot(a, b, c), p], own_sem.at[p]
        )

    for p in range(PIECES):
        own(p).start()

    @pl.loop(0, 4 * line)
    def _(s):
        lhs_copy(s).start()

    acc[...] = jnp.zeros_like(acc)
    meet(line)
    for p in range(PIECES):
        own(p).wait()

    def send(s, p, sem, tok):
        return remote(held.at[s, p], held.at[s, p], sem.at[s, p], recv.at[s, p], tok)

    def to_left(x, p):
        return send(slot(x, b, c), p, left_sem, slot(a - 1, b, c))

    def to_right(x, p):
        return send(slot(x, b, c), p, right_sem, slot(a + 1, b, c))

    def to_row(x, p):
        return send(slot(x, b, c), p, y_sem, slot(a, 1 - b, c))

    def to_core(x, y, p):
        return send(slot(x, y, c), p, core_sem, slot(a, b, 1 - c))

    def arrived(s, p):
        send(s, p, core_sem, slot(a, b, 1 - c)).wait_recv()

    def multiply(s):
        lhs_copy(s).wait()

        for p in range(PIECES):

            @pl.loop(0, piece // tile)
            def _(n):
                start = pl.multiple_of(n * tile, tile)
                columns = pl.ds(pl.multiple_of(p * piece + start, tile), tile)
                acc[:, columns] += jnp.dot(
                    lhs[s], held[s, p, :, pl.ds(start, tile)], preferred_element_type=F32
                )

    def each(d, work):
        for sign in (-1, 1):
            x = a + sign * d
            inside = (x >= 0) & (x < line) & (d >= 0) & ((d > 0) | (sign < 0))
            pl.when(inside)(functools.partial(work, x))

    def line_in(x):
        for p in range(PIECES):

            @pl.when(x != a)
            def _():
                arrived(slot(x, b, c), p)

            @pl.when((x <= a) & (a < line - 1))
            def _():
                to_right(x, p).start()

            @pl.when((x >= a) & (a > 0))
            def _():
                to_left(x, p).start()

            to_row(x, p).start()
            to_core(x, b, p).start()

    def row_in(x):
        for p in range(PIECES):
            arrived(slot(x, 1 - b, c), p)
            to_core(x, 1 - b, p).start()
        multiply(slot(x, 1 - b, c))

    def core_in(y, x):
        for p in range(PIECES):
            arrived(slot(x, y, 1 - c), p)
        multiply(slot(x, y, 1 - c))

    @pl.loop(0, line + 1)
    def _(d):
        each(d, line_in)
        each(d, lambda x: multiply(slot(x, b, c)))
        each(d - 1, functools.partial(core_in, b))
        each(d - 1, row_in)
        each(d - 2, functools.partial(core_in, 1 - b))

    each(line - 1, functools.partial(core_in, 1 - b))

    @pl.loop(0, line)
    def _(x):
        for p in range(PIECES):

            @pl.when((x <= a) & (a < line - 1))
            def _():
                to_right(x, p).wait_send()

            @pl.when((x >= a) & (a > 0))
            def _():
                to_left(x, p).wait_send()

            to_row(x, p).wait_send()
            to_core(x, b, p).wait_send()
            to_core(x, 1 - b, p).wait_send()

    out_ref[...] = acc[...].astype(out_ref.dtype)


def gather_dot(lhs, shard, tok, dtype, collective):
    rows = lhs.shape[0]
    depth, width = shard.shape
    dma = pltpu.SemaphoreType.DMA
    return pl.pallas_call(
        functools.partial(gather_dot_kernel, tok // 4),
        out_shape=jax.ShapeDtypeStruct((rows, width), dtype),
        in_specs=[pl.BlockSpec(memory_space=pl.ANY)] * 2,
        out_specs=pl.BlockSpec(memory_space=pltpu.VMEM),
        scratch_shapes=[
            pltpu.VMEM((tok, PIECES, depth, width // PIECES), BF16),
            pltpu.VMEM((tok, rows, depth), BF16),
            pltpu.VMEM((rows, width), F32),
            dma((tok,)), dma((PIECES,)),
        ]
        + [dma((tok, PIECES))] * 5,
        compiler_params=pltpu.CompilerParams(
            collective_id=collective, has_side_effects=True, vmem_limit_bytes=VMEM_BYTES
        ),
        cost_estimate=pl.CostEstimate(
            flops=2 * rows * width * depth * tok,
            bytes_accessed=2 * rows * depth * tok + 4 * rows * width,
            transcendentals=0,
        ),
    )(lhs, shard)


def dot_scatter_kernel(
    line, act_ref, grad_ref, out_ref,
    core_out, core_in, row_out, row_in, line_out, from_left, from_right,
    core_send, core_recv, row_send, row_recv, line_send, left_recv, right_recv,
):
    a, b, c = place()
    depth, width = out_ref.shape
    piece = width // PIECES
    tile = min(512, piece)
    meet(line)

    def slot(x, y, z):
        return 4 * x + 2 * y + z

    def tiles(p, work):
        @pl.loop(0, piece // tile)
        def _(n):
            start = pl.multiple_of(n * tile, tile)
            work(pl.ds(start, tile), pl.ds(pl.multiple_of(p * piece + start, tile), tile))

    def part(s, columns):
        rows = pl.ds(pl.multiple_of(s * depth, depth), depth)
        return lax.dot_general(
            act_ref[:, rows], grad_ref[:, columns], (((0,), (0,)), ((), ())),
            preferred_element_type=F32,
        )

    def core_copy(k, p):
        return remote(
            core_out.at[k, p], core_in.at[k, p], core_send.at[k, p], core_recv.at[k, p],
            slot(a, b, 1 - c),
        )

    def row_copy(x, p):
        return remote(
            row_out.at[x, p], row_in.at[x, p], row_send.at[x, p], row_recv.at[x, p],
            slot(a, 1 - b, c),
        )

    def right_copy(x, p):
        return remote(
            line_out.at[x, p], from_left.at[x, p], line_send.at[x, p], left_recv.at[x, p],
            slot(a + 1, b, c),
        )

    def left_copy(x, p):
        return remote(
            line_out.at[x, p], from_right.at[x, p], line_send.at[x, p], right_recv.at[x, p],
            slot(a - 1, b, c),
        )

    def each(d, work):
        for sign in (-1, 1):
            x = a + sign * d
            inside = (x >= 0) & (x < line) & (d >= 0) & ((d > 0) | (sign < 0))
            pl.when(inside)(functools.partial(work, x))

    def give_core(y, x):
        k = 2 * x + y
        for p in range(PIECES):

            def work(inner, columns):
                core_out[k, p, :, inner] = part(slot(x, y, 1 - c), columns).astype(BF16)

            tiles(p, work)
            core_copy(k, p).start()

    def give_row(x):
        k = 2 * x + 1 - b
        for p in range(PIECES):
            core_copy(k, p).wait_recv()

            def work(inner, columns):
                total = part(slot(x, 1 - b, c), columns) + core_in[k, p, :, inner].astype(F32)
                row_out[x, p, :, inner] = total.astype(BF16)

            tiles(p, work)
            row_copy(x, p).start()

    def give_line(x):
        k = 2 * x + b
        for p in range(PIECES):
            core_copy(k, p).wait_recv()

            def local(inner, columns):
                out_ref[:, columns] = (
                    part(slot(x, b, c), columns) + core_in[k, p, :, inner].astype(F32)
                )

            def add(ref, inner, columns):
                out_ref[:, columns] += ref[x, p, :, inner].astype(F32)

            def cast(inner, columns):
                line_out[x, p, :, inner] = out_ref[:, columns].astype(BF16)

            tiles(p, local)
            row_copy(x, p).wait_recv()
            tiles(p, functools.partial(add, row_in))

            @pl.when((x >= a) & (a > 0))
            def _():
                right_copy(x, p).wait_recv()
                tiles(p, functools.partial(add, from_left))

            @pl.when((x <= a) & (a < line - 1))
            def _():
                left_copy(x, p).wait_recv()
                tiles(p, functools.partial(add, from_right))

            @pl.when(x != a)
            def _():
                tiles(p, cast)

            @pl.when(x > a)
            def _():
                right_copy(x, p).start()

            @pl.when(x < a)
            def _():
                left_copy(x, p).start()

    @pl.loop(0, line + 1)
    def _(i):
        d = line - 1 - i
        each(d, functools.partial(give_core, 1 - b))
        each(d, give_row)
        each(d, functools.partial(give_core, b))

        @pl.when(i > 0)
        def _():
            each(d + 1, give_line)

    @pl.loop(0, line)
    def _(x):
        for p in range(PIECES):
            core_copy(2 * x, p).wait_send()
            core_copy(2 * x + 1, p).wait_send()
            row_copy(x, p).wait_send()

            @pl.when(x > a)
            def _():
                right_copy(x, p).wait_send()

            @pl.when(x < a)
            def _():
                left_copy(x, p).wait_send()


def dot_scatter(activations, d_pred, tok, collective):
    tokens, features = activations.shape
    width = d_pred.shape[1]
    depth = features // tok
    line = tok // 4
    dma = pltpu.SemaphoreType.DMA

    def slots(n):
        return pltpu.VMEM((n, PIECES, depth, width // PIECES), BF16)

    return pl.pallas_call(
        functools.partial(dot_scatter_kernel, line),
        out_shape=jax.ShapeDtypeStruct((depth, width), F32),
        in_specs=[pl.BlockSpec(memory_space=pltpu.VMEM)] * 2,
        out_specs=pl.BlockSpec(memory_space=pltpu.VMEM),
        scratch_shapes=[
            slots(2 * line), slots(2 * line), slots(line), slots(line), slots(line),
            slots(line), slots(line),
            dma((2 * line, PIECES)), dma((2 * line, PIECES)),
        ]
        + [dma((line, PIECES))] * 5,
        compiler_params=pltpu.CompilerParams(
            collective_id=collective, has_side_effects=True, vmem_limit_bytes=VMEM_BYTES
        ),
        cost_estimate=pl.CostEstimate(
            flops=2 * tokens * features * width,
            bytes_accessed=2 * tokens * (features + width),
            transcendentals=0,
        ),
    )(activations, d_pred)


def adam_step(weight, first, second, grad):
    moment1 = 0.9 * first + 0.1 * grad
    moment2 = 0.95 * second + 0.05 * grad * grad
    return weight - 0.02 * (moment1 / (1.0 - 0.9**10)) / (
        jnp.sqrt(moment2 / (1.0 - 0.95**10)) + 1e-08
    )


def per_device(tok, col, activations, targets, map_weight, first_moment, second_moment, down_weight):
    target32 = targets.astype(F32)
    down_full = lax.all_gather(down_weight, "col", axis=1, tiled=True)
    predicted = gather_dot(activations, map_weight.astype(BF16), tok, F32, 1)
    own = jnp.stack(
        [
            jnp.sum(predicted * target32, axis=1),
            jnp.sum(predicted * predicted, axis=1),
            jnp.sum(target32 * target32, axis=1),
        ]
    )
    sums = own
    for shift in range(1, col):
        sums += lax.ppermute(own, "col", [(k, (k + shift) % col) for k in range(col)])
    inner, pred_sq, target_sq = sums[0], sums[1], sums[2]
    pred_norm = jnp.sqrt(pred_sq + 1e-06)
    targ_norm = jnp.sqrt(target_sq + 1e-06)
    scale = 1.0 / (pred_norm * targ_norm)
    coef = inner * scale / (pred_norm * pred_norm)
    d_pred = (coef[:, None] * predicted - scale[:, None] * target32).astype(BF16)
    grad = dot_scatter(activations, d_pred, tok, 2)
    new_map = adam_step(map_weight, first_moment, second_moment, grad)
    joined = gather_dot(down_full, new_map.astype(BF16), tok, BF16, 3)
    return (new_map, joined)


def solution(mesh):
    split = P("tok", "col")
    return jax.shard_map(
        functools.partial(per_device, mesh.shape["tok"], mesh.shape["col"]),
        mesh=mesh,
        in_specs=(P("tok", None),) + (split,) * 5,
        out_specs=(split, split),
        check_vma=False,
    )
```

time: 378 us -> 360 us (0.952)
  Pallas kernels: 330 us -> 320 us
  blocking collectives: 8.15 us -> 0 us
  other arithmetic: 19.8 us -> 15.9 us
    psum x1 -> x0, blocking collectives: 8.15 us -> none  [per_device(): lax.psum(jnp.stack([jnp.sum(predicted * target32, axis=1), jnp.sum(predic...]
    pallas_call x1, Pallas kernels: 109 us -> 103 us  [dot_scatter(): pl.pallas_call(functools.partial(dot_scatter_kernel, line), out_shape=jax...]
    pallas_call x2, Pallas kernels: 221 us -> 216 us  [gather_dot(): pl.pallas_call(functools.partial(gather_dot_kernel, tok // 4), out_shape=...]
    convert_element_type x1, other arithmetic: 6.93 us -> 2.81 us  [per_device(): (coef[:, None] * predicted - scale[:, None] * target32).astype(BF16)]
  transfers between devices with their start and end apart: 1 -> 2, of which waited for: 0 -> 1; matrix products, arithmetic and copies ran while one was open for 5% -> 4% of each run, Pallas kernels for 58% -> 59%
where the time goes in v2:
time: 360 us
  Pallas kernels  320 us (89%)
  other arithmetic  15.9 us (4%)
  between operations  14.1 us (4%)
  local copies, waits for them, and re-layouts  5.23 us (1%)
    pallas_call x2, Pallas kernels, gather_dot(): pl.pallas_call(functools.partial(gather_dot_kernel, tok // 4), out_shape=...  216 us
    pallas_call x1, Pallas kernels, dot_scatter(): pl.pallas_call(functools.partial(dot_scatter_kernel, line), out_shape=jax...  103 us
  transfers between devices with their start and end apart: 2, of which 1 were waited for; matrix products, arithmetic and copies ran while one was open for 4% of the time, Pallas kernels for 59%

profile of v2, /device:TPU:0, one launch (start us, length us, event | category | flops | bytes accessed | tf_op | source)
XLA Modules:
  0.0 359.6 jit_solution(17714015498744719322)
XLA Ops:
  7.2 0.0 copy-start.2
  7.2 0.0 all-gather.2.cloned.1.call-start
  7.2 0.7 all-gather.2.cloned.1.call-update
  7.9 0.8 copy-done.2
  8.8 1.1 convert_element_type.12.shard_ref
  9.9 110.4 %shard_map.77 = f32[1024,2048]{1,0:T(8,128)} custom-call(bf16[1024,4096]{1,0:T(8,128)(2,1)} %act_ref.1, bf16[256,2048]{1,0:T(8,128)(2,1)} %convert_element_type.12.shard_ref), custom_call_target="tpu_custom_call" | custom-call | flops 17179869184 | bytes 16777216 | tf_op jit(solution)/shard_map/pallas_call | solution.py:176
  120.3 0.0 copy-start
  120.3 0.0 copy-start.1
  120.3 5.9 %fusion = (f32[1024]{0:T(1024)S(1)}, f32[1024]{0:T(1024)S(1)}, f32[1024]{0:T(1024)S(1)}) fusion(f32[1024,2048]{1,0:T(8,128)} %shard_map.77, bf16[1024,2048]{1,0:T(8,128)(2,1)} %param.7), kind=kLoop, calls=%fused_computation.3 | loop fusion | flops 14676992 | bytes 12595200 | tf_op jit(solution)/shard_map/reduce_sum | solution.py:393
  126.3 1.5 collective-permute-start
  127.8 2.3 collective-permute-done
  130.2 0.0 copy-done
  130.2 0.0 copy-done.1
  130.2 2.8 fusion.3.grad_ref
  133.0 103.5 %shard_map.78 = f32[256,2048]{1,0:T(8,128)} custom-call(bf16[1024,4096]{1,0:T(8,128)(2,1)} %act_ref.1, bf16[1024,2048]{1,0:T(8,128)(2,1)} %fusion.3.grad_ref), custom_call_target="tpu_custom_call" | custom-call | flops 17179869184 | bytes 12582912 | tf_op jit(solution)/shard_map/pallas_call | solution.py:357
  236.5 5.9 %fusion.16 = (bf16[256,2048]{1,0:T(8,128)(2,1)}, f32[256,2048]{1,0:T(8,128)}) fusion(f32[256,2048]{1,0:T(8,128)S(1)} %copy-done.2, f32[256,2048]{1,0:T(8,128)} %shard_map.78, f32[256,2048]{1,0:T(8,128)} %param.10, f32[256,2048]{1,0:T(8,128)} %param.9), kind=kLoop, calls=%fused_computation.25 | loop fusion | flops 6815744 | bytes 11534336 | tf_op jit(solution)/shard_map/convert_element_type | solution.py:409
  242.4 0.0 all-gather.2.cloned.1.call-done.lhs_ref
  242.4 106.0 %shard_map.79 = bf16[896,2048]{1,0:T(8,128)(2,1)} custom-call(bf16[896,4096]{1,0:T(8,128)(2,1)} %all-gather.2.cloned.1.call-done.lhs_ref, bf16[256,2048]{1,0:T(8,128)(2,1)} %get-tuple-element.5.shard_ref), custom_call_target="tpu_custom_call" | custom-call | flops 15032385536 | bytes 14680064 | tf_op jit(solution)/shard_map/pallas_call | solution.py:176
  348.4 4.4 %copy.9 = bf16[896,2048]{1,0:T(8,128)(2,1)} copy(bf16[896,2048]{1,0:T(8,128)(2,1)} %shard_map.79) | data formatting | bytes 7340032
  (4 shorter events, 0.1 us)
Async XLA Ops:
  7.2 1.6 copy-start.2
  7.2 235.2 %all-gather.2.cloned.1.call-start = ((), (), s32[]{:S(2)}) async-start(), calls=%async_computation | async-start | bytes 11010048 | tf_op jit(solution)/shard_map/all_gather | solution.py:389
  120.3 9.8 %copy-start = (f32[1024,2048]{1,0:T(8,128)S(1)}, f32[1024,2048]{1,0:T(8,128)}, u32[]{:S(2)}) copy-start(f32[1024,2048]{1,0:T(8,128)} %shard_map.77) | copy-start | bytes 25165828
  120.3 9.8 %copy-start.1 = (bf16[1024,2048]{1,0:T(8,128)(2,1)S(1)}, bf16[1024,2048]{1,0:T(8,128)(2,1)}, u32[]{:S(2)}) copy-start(bf16[1024,2048]{1,0:T(8,128)(2,1)} %param.7) | copy-start | bytes 12582916
  126.3 3.8 %collective-permute-start = (f32[3,1024]{1,0:T(4,128)S(1)}, f32[3,1024]{1,0:T(4,128)S(1)}, u32[]{:S(2)}, u32[]{:S(2)}) collective-permute-start(f32[3,1024]{1,0:T(4,128)S(1)} %pad_maximum_fusion), channel_id=1, source_target_pairs={{0,1},{1,0},{2,3},{3,2},{4,5},{5,4},{6,7},{7,6},{8,9},{9,8},{10,11... | collective-permute-start | bytes 36872 | tf_op jit(solution)/shard_map/ppermute | solution.py:400
Sparse Core Ops, SparseCore 0:
  9.6 94.8 all-gather.1
